TPU v7x, 32 devices: a whole 2x2x4 slice. The times are simulated.
32 devices in a mesh: grp: 2 (over y), row: 4 (over z), col: 4 (over x, core).
Axes of the slice: x: 2, y: 2, z: 4, core: 2. Of those that a mesh axis runs over, the one named last changes fastest.
Arguments:
- activations: bfloat16 [64, 6144], P(('grp', 'row'), 'col'), parts along dimension 0, may hold values from -6 to 6
- up_weight: bfloat16 [6144, 49152], P('col', 'row'), may hold values from -0.078125 to 0.078125
- up_bias: float32 [49152], P('row'), may hold values from -3 to 3
- cotangent: bfloat16 [64, 49152], P(('grp', 'col'), 'row'), parts along dimension 0, may hold values from -6 to 6
Outputs:
- hidden: bfloat16 [64, 49152], P(('grp', 'col'), 'row'), parts along dimension 0
- act_grad: bfloat16 [64, 6144], P(('grp', 'row'), 'col'), parts along dimension 0
- weight_grad: bfloat16 [12288, 49152], P(('grp', 'col'), 'row'), parts along dimension 0
- bias_grad: float32 [98304], P(('grp', 'row')), parts along dimension 0
There are 2 independent parts, one for each index of `grp`. A program takes and returns all parts, laid end to end along the dimension named above; an argument that names none is the same for every part. Nothing has to cross between parts.
All inputs are finite; a program needn't handle non-finite values.
Results may differ from a plain program's by a relative error of at most 0.0049.
Values may be sent and summed in bfloat16 or wider, within the bound.
A program may use at most 256 MiB of HBM per device.

v0:
```python
import jax
import jax.numpy as jnp
from jax import lax
from jax.sharding import PartitionSpec as P

root_coef = 0.7978845608028654
cube_coef = 0.044715


def gelu_tanh(value):
    inner = root_coef * (value + cube_coef * value * value * value)
    return 0.5 * value * (1.0 + jnp.tanh(inner))


def gelu_slope(value):
    inner = root_coef * (value + cube_coef * value * value * value)
    tanh_val = jnp.tanh(inner)
    return 0.5 * (1.0 + tanh_val) + 0.5 * value * (1.0 - tanh_val * tanh_val) * root_coef * (
        1.0 + 3.0 * cube_coef * value * value
    )


def per_device(activations, up_weight, up_bias, cotangent):
    gathered = lax.all_gather(activations, "row", axis=0, tiled=True)
    partial_value = jnp.dot(gathered, up_weight, preferred_element_type=jnp.float32)
    pre = lax.psum_scatter(partial_value, "col", scatter_dimension=0, tiled=True) + up_bias
    hidden = gelu_tanh(pre).astype(jnp.bfloat16)
    grad_own = (cotangent.astype(jnp.float32) * gelu_slope(pre)).astype(jnp.bfloat16)
    grad_pre = lax.all_gather(grad_own, "col", axis=0, tiled=True)
    bias_grad = jnp.sum(grad_pre.astype(jnp.float32), axis=0)
    weight_sum = lax.dot_general(
        gathered, grad_pre, (((0,), (0,)), ((), ())), preferred_element_type=jnp.float32
    )
    weight_grad = weight_sum.astype(jnp.bfloat16)
    act_grad = lax.psum_scatter(
        lax.dot_general(
            grad_pre, up_weight, (((1,), (1,)), ((), ())), preferred_element_type=jnp.float32
        ),
        "row",
        scatter_dimension=0,
        tiled=True,
    ).astype(jnp.bfloat16)
    return (hidden, act_grad, weight_grad, bias_grad)


def solution(mesh):
    in_specs = (P(("grp", "row"), "col"), P("col", "row"), P("row"), P(("grp", "col"), "row"))
    out_specs = (
        P(("grp", "col"), "row"),
        P(("grp", "row"), "col"),
        P(("grp", "col"), "row"),
        P(("grp", "row")),
    )
    return jax.shard_map(
        per_device, mesh=mesh, in_specs=in_specs, out_specs=out_specs, check_vma=False
    )
```

profile of v0, /device:TPU:0, one launch (start us, length us, event | category | flops | bytes accessed | tf_op | source)
XLA Modules:
  0.0 169.8 jit_solution(11756558600709857724)
XLA Ops:
  7.2 0.0 copy-start
  7.2 0.0 copy-start.1
  7.2 0.0 reduce-scatter.3.cloned.1.call-start
  7.2 15.4 %all_gather.6 = bf16[32,1536]{1,0:T(8,128)(2,1)S(1)} all-gather(bf16[8,1536]{1,0:T(8,128)(2,1)} %param.4), channel_id=1, replica_groups=mesh['grp'=2,'row'=4,'col'=4] {'row'}, dimensions={0}, use_global_device_ids=true | all-gather | bytes 122880 | tf_op jit(solution)/shard_map/all_gather | solution.py:24
  22.6 16.3 %fusion.8 = f32[32,12288]{1,0:T(8,128)} fusion(bf16[32,1536]{1,0:T(8,128)(2,1)S(1)} %all_gather.6, bf16[1536,12288]{1,0:T(8,128)(2,1)} %param.5), kind=kOutput, calls=%fused_computation.13 | convolution fusion | flops 1207959552 | bytes 39419904 | tf_op jit(solution)/shard_map/dot_general | solution.py:25
  38.9 0.0 reduce-scatter.3.cloned.1.call-update
  39.0 0.0 reduce-scatter.5.cloned.1.call-start
  39.0 29.4 %reduce-scatter.3.cloned.1.call-done = f32[8,12288]{1,0:T(8,128)} async-done(((f32[32,12288]{1,0:T(8,128)}), f32[8,12288]{1,0:T(8,128)}) %reduce-scatter.3.cloned.1.call-update) | async-done | bytes 393232 | tf_op jit(solution)/shard_map/reduce_scatter | solution.py:26
  68.4 0.0 copy-done
  68.4 0.0 copy-done.1
  68.4 2.0 %fusion.7 = (bf16[8,12288]{1,0:T(8,128)(2,1)S(1)}, bf16[8,12288]{1,0:T(8,128)(2,1)}) fusion(bf16[8,12288]{1,0:T(8,128)(2,1)S(1)} %copy-done, f32[8,12288]{1,0:T(8,128)} %reduce-scatter.3.cloned.1.call-done, f32[12288]{0:T(1024)S(1)} %copy-done.1), kind=kLoop, calls=%fused_computation.11 | loop fusion | flops 2260992 | bytes 1032192 | tf_op jit(solution)/shard_map/convert_element_type | solution.py:28
  70.4 8.2 %all_gather.7 = bf16[32,12288]{1,0:T(8,128)(2,1)S(1)} all-gather(bf16[8,12288]{1,0:T(8,128)(2,1)S(1)} %get-tuple-element.8), channel_id=1, replica_groups=mesh['grp'=2,'row'=4,'col'=4] {'col'}, dimensions={0}, use_global_device_ids=true | all-gather | bytes 983040 | tf_op jit(solution)/shard_map/all_gather | solution.py:29
  78.6 17.5 %fusion.9 = f32[32,1536]{1,0:T(8,128)} fusion(bf16[32,12288]{1,0:T(8,128)(2,1)S(1)} %all_gather.7, bf16[1536,12288]{1,0:T(8,128)(2,1)} %param.5), kind=kOutput, calls=%fused_computation.14 | convolution fusion | flops 1207959552 | bytes 38731776 | tf_op jit(solution)/shard_map/dot_general | solution.py:36
  96.1 0.0 reduce-scatter.5.cloned.1.call-update
  96.1 16.1 %fusion = bf16[1536,12288]{0,1:T(8,128)(2,1)} fusion(bf16[32,12288]{1,0:T(8,128)(2,1)S(1)} %all_gather.7, bf16[32,1536]{1,0:T(8,128)(2,1)S(1)} %all_gather.6), kind=kOutput, calls=%fused_computation.1 | convolution fusion | flops 1226833920 | bytes 38633472 | tf_op jit(solution)/shard_map/dot_general | solution.py:31
  112.2 48.5 %copy.8 = bf16[1536,12288]{1,0:T(8,128)(2,1)} copy(bf16[1536,12288]{0,1:T(8,128)(2,1)} %fusion) | data formatting | bytes 75497472
  160.8 0.8 convert_reduce_fusion
  161.6 0.0 reduce-scatter.5.cloned.1.call-done
  161.6 1.4 convert_element_type.24
Async XLA Ops:
  7.2 61.3 %copy-start = (bf16[8,12288]{1,0:T(8,128)(2,1)S(1)}, bf16[8,12288]{1,0:T(8,128)(2,1)}, u32[]{:S(2)}) copy-start(bf16[8,12288]{1,0:T(8,128)(2,1)} %param.7) | copy-start | bytes 589828
  7.2 61.3 %copy-start.1 = (f32[12288]{0:T(1024)S(1)}, f32[12288]{0:T(1024)}, u32[]{:S(2)}) copy-start(f32[12288]{0:T(1024)} %param.6) | copy-start | bytes 147460
  7.2 61.2 %reduce-scatter.3.cloned.1.call-start = ((), (), s32[]{:S(2)}) async-start(), calls=%async_computation.2 | async-start | bytes 1966080 | tf_op jit(solution)/shard_map/reduce_scatter | solution.py:26
  39.0 122.6 %reduce-scatter.5.cloned.1.call-start = ((), (), s32[]{:S(2)}) async-start(), calls=%async_computation.3 | async-start | bytes 245760 | tf_op jit(solution)/shard_map/reduce_scatter | solution.py:35
Sparse Core Ops, SparseCore 0:
  39.1 29.2 reduce-scatter.2
  96.2 19.7 reduce-scatter.4
where the time goes:
time: 171 us; the launch traced here: 170 us
  matrix products  49.9 us (29%)
  local copies, waits for them, and re-layouts  48.5 us (28%)
  waiting for transfers between devices  29.4 us (17%)
  blocking collectives  23.6 us (14%)
  between operations  14.1 us (8%)
  other arithmetic  4.18 us (2%)
    unnamed x5, local copies, waits for them, and re-layouts  48.5 us
    reduce_scatter x1, waiting for transfers between devices, per_device(): lax.psum_scatter(partial_value, 'col', scatter_dimension=0, tiled=True)  29.4 us
    dot_general x1, matrix products, per_device(): lax.dot_general(grad_pre, up_weight, (((1,), (1,)), ((), ())), preferred_...  17.5 us
    dot_general x1, matrix products, per_device(): jnp.dot(gathered, up_weight, preferred_element_type=jnp.float32)  16.3 us
    dot_general x1, matrix products, per_device(): lax.dot_general(gathered, grad_pre, (((0,), (0,)), ((), ())), preferred_e...  16.1 us
    all_gather x1, blocking collectives, per_device(): gathered = lax.all_gather(activations, 'row', axis=0, tiled=True)  15.4 us
    all_gather x1, blocking collectives, per_device(): grad_pre = lax.all_gather(grad_own, 'col', axis=0, tiled=True)  8.18 us
  transfers between devices with their start and end apart: 2, of which 1 were waited for; matrix products, arithmetic and copies ran while one was open for 39% of the time, Pallas kernels for 0%

commit v1 on v0

--- a/solution.py
+++ b/solution.py
@@ -1,10 +1,17 @@
+import functools
+
 import jax
 import jax.numpy as jnp
 from jax import lax
+from jax.experimental import pallas as pl
+from jax.experimental.pallas import tpu as pltpu
 from jax.sharding import PartitionSpec as P
 
 root_coef = 0.7978845608028654
 cube_coef = 0.044715
+MESH = pl.DeviceIdType.MESH
+F32 = jnp.float32
+BF16 = jnp.bfloat16
 
 
 def gelu_tanh(value):
@@ -20,7 +27,7 @@
     )
 
 
-def per_device(activations, up_weight, up_bias, cotangent):
+def general_per_device(activations, up_weight, up_bias, cotangent):
     gathered = lax.all_gather(activations, "row", axis=0, tiled=True)
     partial_value = jnp.dot(gathered, up_weight, preferred_element_type=jnp.float32)
     pre = lax.psum_scatter(partial_value, "col", scatter_dimension=0, tiled=True) + up_bias
@@ -43,6 +50,305 @@
     return (hidden, act_grad, weight_grad, bias_grad)
 
 
+def exchange_kernel(
+    chunks, act, weight, bias, cot,
+    hidden_out, act_grad_out, x_out, grad_out,
+    wbuf, ag, x32, cbuf, bbuf, part, r1, s2, r2, gbuf, g32, hbuf, acc, r3, obuf,
+    w_sem, in_sem, ag_send, ag_recv, s1_send, s1_recv, s2_send, s2_recv,
+    gp_send, gp_recv, gx_send, gx_recv, gf_send, gf_recv, r3_send, r3_recv, out_sem, gout_sem,
+):
+    rows = ag.shape[0]
+    width = wbuf.shape[2]
+    feats = wbuf.shape[1]
+    row = lax.axis_index("row")
+    col = lax.axis_index("col")
+    x = lax.div(col, 2)
+    core = lax.rem(col, 2)
+    mate = 2 * x + (1 - core)
+    across = 2 * (1 - x) + core
+    diag = 2 * (1 - x) + (1 - core)
+
+    def w_copy(k):
+        return pltpu.make_async_copy(
+            weight.at[:, pl.ds(pl.multiple_of(k * width, 128), width)], wbuf.at[k], w_sem.at[k]
+        )
+
+    own_copy = pltpu.make_async_copy(act, ag.at[row], in_sem.at[0])
+    own_copy.start()
+    w_copy(0).start()
+    cot_copy = pltpu.make_async_copy(cot, cbuf, in_sem.at[1])
+    bias_copy = pltpu.make_async_copy(bias, bbuf, in_sem.at[2])
+
+    barrier = pltpu.get_barrier_semaphore()
+    for d in range(1, rows):
+        pl.semaphore_signal(
+            barrier, inc=1, device_id={"row": lax.rem(row + d, rows)}, device_id_type=MESH
+        )
+    for peer in (mate, across):
+        pl.semaphore_signal(barrier, inc=1, device_id={"col": peer}, device_id_type=MESH)
+    pl.semaphore_wait(barrier, rows + 1)
+
+    ag_copies = [
+        pltpu.make_async_remote_copy(
+            src_ref=act, dst_ref=ag.at[row], send_sem=ag_send.at[d - 1], recv_sem=ag_recv.at[d - 1],
+            device_id={"row": lax.rem(row + d, rows)}, device_id_type=MESH,
+        )
+        for d in range(1, rows)
+    ]
+    for copy in ag_copies:
+        copy.start()
+    for k in range(1, chunks):
+        w_copy(k).start()
+    cot_copy.start()
+    bias_copy.start()
+
+    own_copy.wait()
+    for copy in ag_copies:
+        copy.wait_recv()
+    x32[...] = jnp.concatenate([ag[i].astype(F32) for i in range(rows)], axis=0).astype(BF16)
+    x_copy = pltpu.make_async_copy(x32, x_out, out_sem.at[0])
+    x_copy.start()
+    acc[...] = jnp.zeros_like(acc)
+    cot_copy.wait()
+    bias_copy.wait()
+
+    def s1_copy(k):
+        return pltpu.make_async_remote_copy(
+            src_ref=part.at[k, 1 - core], dst_ref=r1.at[k], send_sem=s1_send.at[k],
+            recv_sem=s1_recv.at[k], device_id={"col": mate}, device_id_type=MESH,
+        )
+
+    def s2_copy(k):
+        return pltpu.make_async_remote_copy(
+            src_ref=s2.at[k], dst_ref=r2.at[k], send_sem=s2_send.at[k],
+            recv_sem=s2_recv.at[k], device_id={"col": across}, device_id_type=MESH,
+        )
+
+    def gp_copy(k):
+        return pltpu.make_async_remote_copy(
+            src_ref=gbuf.at[k, col], dst_ref=gbuf.at[k, col], send_sem=gp_send.at[k],
+            recv_sem=gp_recv.at[k], device_id={"col": mate}, device_id_type=MESH,
+        )
+
+    def gx_copy(k):
+        return pltpu.make_async_remote_copy(
+            src_ref=gbuf.at[k, col], dst_ref=gbuf.at[k, col], send_sem=gx_send.at[k],
+            recv_sem=gx_recv.at[k], device_id={"col": across}, device_id_type=MESH,
+        )
+
+    def gf_copy(k):
+        return pltpu.make_async_remote_copy(
+            src_ref=gbuf.at[k, across], dst_ref=gbuf.at[k, across], send_sem=gf_send.at[k],
+            recv_sem=gf_recv.at[k], device_id={"col": mate}, device_id_type=MESH,
+        )
+
+    def g_out(k):
+        return pltpu.make_async_copy(g32.at[k], grad_out.at[k], gout_sem.at[k])
+
+    tile = 512 if width % 512 == 0 else 256
+    ftile = 512 if feats % 512 == 0 else 256
+
+    def dot_up(k):
+        w_copy(k).wait()
+
+        def body(i, carry):
+            cols = pl.ds(pl.multiple_of(i * tile, tile), tile)
+            out = jnp.dot(x32[...], wbuf[k, :, cols], preferred_element_type=F32)
+            for j in range(4):
+                part[k, j % 2, j // 2, :, cols] = out[8 * j : 8 * j + 8]
+            return carry
+
+        lax.fori_loop(0, width // tile, body, 0)
+        s1_copy(k).start()
+
+    def pair_sum(k):
+        s1_copy(k).wait_recv()
+        s2[k] = part[k, core, 1 - x] + r1[k, 1 - x]
+        s2_copy(k).start()
+
+    def activate(k):
+        s2_copy(k).wait_recv()
+        cols = pl.ds(pl.multiple_of(k * width, 128), width)
+        pre = part[k, core, x] + r1[k, x] + r2[k] + bbuf[:, cols]
+        hbuf[:, cols] = gelu_tanh(pre).astype(BF16)
+        gbuf[k, col] = (cbuf[:, cols].astype(F32) * gelu_slope(pre)).astype(BF16)
+        gx_copy(k).start()
+        gp_copy(k).start()
+
+    def forward(k):
+        gx_copy(k).wait_recv()
+        gf_copy(k).start()
+
+    def dot_down(k):
+        gp_copy(k).wait_recv()
+        gf_copy(k).wait_recv()
+        grad = jnp.concatenate([gbuf[k, i].astype(F32) for i in range(4)], axis=0).astype(BF16)
+        g32[k] = grad
+        g_out(k).start()
+
+        def body(i, carry):
+            feat = pl.ds(pl.multiple_of(i * ftile, ftile), ftile)
+            acc[:, feat] += lax.dot_general(
+                g32[k], wbuf[k, feat, :], (((1,), (1,)), ((), ())), preferred_element_type=F32
+            )
+            return carry
+
+        lax.fori_loop(0, feats // ftile, body, 0)
+
+    def stages(t, carry):
+        for lag, stage in enumerate((dot_up, pair_sum, activate, forward, dot_down)):
+            k = t - lag
+            pl.when(jnp.logical_and(k >= 0, k < chunks))(functools.partial(stage, k))
+        return carry
+
+    lax.fori_loop(0, chunks + 4, stages, 0)
+
+    hidden_copy = pltpu.make_async_copy(hbuf, hidden_out, out_sem.at[1])
+    hidden_copy.start()
+    r3_copies = []
+    for d in range(1, rows):
+        to = lax.rem(row + d, rows)
+        copy = pltpu.make_async_remote_copy(
+            src_ref=acc.at[pl.ds(pl.multiple_of(to * 8, 8), 8)], dst_ref=r3.at[d - 1],
+            send_sem=r3_send.at[d - 1], recv_sem=r3_recv.at[d - 1],
+            device_id={"row": to}, device_id_type=MESH,
+        )
+        copy.start()
+        r3_copies.append(copy)
+
+    def drain(k, carry):
+        s1_copy(k).wait_send()
+        s2_copy(k).wait_send()
+        gp_copy(k).wait_send()
+        gx_copy(k).wait_send()
+        gf_copy(k).wait_send()
+        g_out(k).wait()
+        return carry
+
+    lax.fori_loop(0, chunks, drain, 0)
+    for copy in ag_copies:
+        copy.wait_send()
+    x_copy.wait()
+    total = acc[pl.ds(pl.multiple_of(row * 8, 8), 8)]
+    for d, copy in enumerate(r3_copies):
+        copy.wait_recv()
+        total += r3[d]
+    obuf[...] = total.astype(BF16)
+    act_copy = pltpu.make_async_copy(obuf, act_grad_out, out_sem.at[2])
+    act_copy.start()
+    for copy in r3_copies:
+        copy.wait_send()
+    hidden_copy.wait()
+    act_copy.wait()
+
+
+def outer_kernel(x_ref, grad_ref, hidden_in, act_in, w_ref, bias_ref, hidden_out, act_out, xt, sems):
+    k, i = pl.program_id(0), pl.program_id(1)
+    last = jnp.logical_and(k == pl.num_programs(0) - 1, i == pl.num_programs(1) - 1)
+    copies = (
+        pltpu.make_async_copy(hidden_in, hidden_out, sems.at[0]),
+        pltpu.make_async_copy(act_in, act_out, sems.at[1]),
+    )
+
+    @pl.when(jnp.logical_and(k == 0, i == 0))
+    def _():
+        for copy in copies:
+            copy.start()
+        xt[...] = jnp.transpose(x_ref[...].astype(F32)).astype(BF16)
+
+    @pl.when(i == 0)
+    def _():
+        bias_ref[...] = jnp.sum(grad_ref[0].astype(F32), axis=0, keepdims=True)
+
+    height = w_ref.shape[0]
+    step = 128
+
+    def body(n, carry):
+        at = pl.multiple_of(n * step, step)
+        lhs = xt[pl.ds(pl.multiple_of(i * height + at, step), step), :]
+        w_ref[pl.ds(at, step), :] = jnp.dot(
+            lhs, grad_ref[0], preferred_element_type=F32
+        ).astype(BF16)
+        return carry
+
+    lax.fori_loop(0, height // step, body, 0)
+
+    @pl.when(last)
+    def _():
+        for copy in copies:
+            copy.wait()
+
+
+def fast_per_device(activations, up_weight, up_bias, cotangent, *, rows, chunks):
+    feats, hidden_units = up_weight.shape
+    width = hidden_units // chunks
+    any_spec = pl.BlockSpec(memory_space=pl.ANY)
+    dma = pltpu.SemaphoreType.DMA
+    hidden, act_grad, x_all, grad_all = pl.pallas_call(
+        functools.partial(exchange_kernel, chunks),
+        out_shape=(
+            jax.ShapeDtypeStruct((8, hidden_units), BF16),
+            jax.ShapeDtypeStruct((8, feats), BF16),
+            jax.ShapeDtypeStruct((32, feats), BF16),
+            jax.ShapeDtypeStruct((chunks, 32, width), BF16),
+        ),
+        in_specs=[any_spec] * 4,
+        out_specs=(any_spec,) * 4,
+        scratch_shapes=[
+            pltpu.VMEM((chunks, feats, width), BF16),
+            pltpu.VMEM((rows, 8, feats), BF16),
+            pltpu.VMEM((32, feats), BF16),
+            pltpu.VMEM((8, hidden_units), BF16),
+            pltpu.VMEM((1, hidden_units), F32),
+            pltpu.VMEM((chunks, 2, 2, 8, width), F32),
+            pltpu.VMEM((chunks, 2, 8, width), F32),
+            pltpu.VMEM((chunks, 8, width), F32),
+            pltpu.VMEM((chunks, 8, width), F32),
+            pltpu.VMEM((chunks, 4, 8, width), BF16),
+            pltpu.VMEM((chunks, 32, width), BF16),
+            pltpu.VMEM((8, hidden_units), BF16),
+            pltpu.VMEM((32, feats), F32),
+            pltpu.VMEM((rows - 1, 8, feats), F32),
+            pltpu.VMEM((8, feats), BF16),
+            dma((chunks,)), dma((3,)), dma((rows - 1,)), dma((rows - 1,)),
+            dma((chunks,)), dma((chunks,)), dma((chunks,)), dma((chunks,)),
+            dma((chunks,)), dma((chunks,)), dma((chunks,)), dma((chunks,)),
+            dma((chunks,)), dma((chunks,)), dma((rows - 1,)), dma((rows - 1,)),
+            dma((3,)), dma((chunks,)),
+        ],
+        compiler_params=pltpu.CompilerParams(
+            collective_id=0, has_side_effects=True, vmem_limit_bytes=56 * 1024 * 1024
+        ),
+    )(activations, up_weight, up_bias.reshape(1, hidden_units), cotangent)
+
+    split = 2
+    weight_grad, bias_grad, hidden, act_grad = pl.pallas_call(
+        outer_kernel,
+        grid=(chunks, split),
+        out_shape=(
+            jax.ShapeDtypeStruct((feats, hidden_units), BF16),
+            jax.ShapeDtypeStruct((1, hidden_units), F32),
+            jax.ShapeDtypeStruct((8, hidden_units), BF16),
+            jax.ShapeDtypeStruct((8, feats), BF16),
+        ),
+        in_specs=[
+            pl.BlockSpec((32, feats), lambda k, i: (0, 0)),
+            pl.BlockSpec((1, 32, width), lambda k, i: (k, 0, 0)),
+            any_spec,
+            any_spec,
+        ],
+        out_specs=(
+            pl.BlockSpec((feats // split, width), lambda k, i: (i, k)),
+            pl.BlockSpec((1, width), lambda k, i: (0, k)),
+            any_spec,
+            any_spec,
+        ),
+        scratch_shapes=[pltpu.VMEM((feats, 32), BF16), dma((2,))],
+        compiler_params=pltpu.CompilerParams(vmem_limit_bytes=40 * 1024 * 1024),
+    )(x_all, grad_all, hidden, act_grad)
+    return hidden, act_grad, weight_grad, bias_grad.reshape(hidden_units)
+
+
 def solution(mesh):
     in_specs = (P(("grp", "row"), "col"), P("col", "row"), P("row"), P(("grp", "col"), "row"))
     out_specs = (
@@ -51,6 +357,26 @@
         P(("grp", "col"), "row"),
         P(("grp", "row")),
     )
+    rows, cols = mesh.shape["row"], mesh.shape["col"]
+
+    def per_device(activations, up_weight, up_bias, cotangent):
+        feats, hidden_units = up_weight.shape
+        chunks = 8
+        fits = (
+            rows == 4
+            and cols == 4
+            and activations.shape[0] == 8
+            and cotangent.shape[0] == 8
+            and feats % 256 == 0
+            and hidden_units % (chunks * 256) == 0
+            and feats * hidden_units <= 1536 * 12288
+        )
+        if fits:
+            return fast_per_device(
+                activations, up_weight, up_bias, cotangent, rows=rows, chunks=chunks
+            )
+        return general_per_device(activations, up_weight, up_bias, cotangent)
+
     return jax.shard_map(
         per_device, mesh=mesh, in_specs=in_specs, out_specs=out_specs, check_vma=False
     )

time: 171 us -> 82.8 us (0.48)
  Pallas kernels: 0 us -> 78.2 us
  matrix products: 49.9 us -> 0 us
  local copies, waits for them, and re-layouts: 48.5 us -> 3.68 us
  waiting for transfers between devices: 29.4 us -> 0 us
  blocking collectives: 23.6 us -> 0 us
  between operations: 14.1 us -> 0.65 us
  other arithmetic: 4.18 us -> 0 us
    pallas_call x0 -> x2, Pallas kernels: none -> 78.2 us  [the longest x1 53.1 us: fast_per_device(): pl.pallas_call(functools.partial(exchange_kernel, chunks), out_shape=(jax...]
    dot_general x3 -> x0, matrix products: 49.9 us -> none  [the longest x1 17.5 us: per_device(): lax.dot_general(grad_pre, up_weight, (((1,), (1,)), ((), ())), preferred_...]
    unnamed x5 -> x8, local copies, waits for them, and re-layouts: 48.5 us -> 3.68 us
    reduce_scatter x2 -> x0, waiting for transfers between devices: 29.4 us -> none  [the longest x1 29.4 us: per_device(): lax.psum_scatter(partial_value, 'col', scatter_dimension=0, tiled=True)]
    all_gather x2 -> x0, blocking collectives: 23.6 us -> none  [the longest x1 15.4 us: per_device(): gathered = lax.all_gather(activations, 'row', axis=0, tiled=True)]
    convert_element_type x2 -> x0, other arithmetic: 3.38 us -> none  [the longest x1 1.97 us: per_device(): (cotangent.astype(jnp.float32) * gelu_slope(pre)).astype(jnp.bfloat16)]
  transfers between devices with their start and end apart: 2 -> 0, of which waited for: 1 -> 0; matrix products, arithmetic and copies ran while one was open for 39% -> 0% of each run, Pallas kernels for 0% -> 0%
where the time goes in v1:
time: 82.8 us; the launch traced here: 82.5 us
  Pallas kernels  78.2 us (94%)
  local copies, waits for them, and re-layouts  3.68 us (4%)
    pallas_call x1, Pallas kernels, fast_per_device(): pl.pallas_call(functools.partial(exchange_kernel, chunks), out_shape=(jax...  53.1 us
    pallas_call x1, Pallas kernels, fast_per_device(): pl.pallas_call(outer_kernel, grid=(chunks, split), out_shape=(jax.ShapeDt...  25.1 us
    unnamed x8, local copies, waits for them, and re-layouts  3.68 us

profile of v1, /device:TPU:0, one launch (start us, length us, event | category | flops | bytes accessed | tf_op | source)
XLA Modules:
  0.0 82.5 jit_solution(18138656949177013213)
XLA Ops:
  0.6 53.1 %shard_map.75 = (bf16[8,12288]{1,0:T(8,128)(2,1)}, bf16[8,1536]{1,0:T(8,128)(2,1)}, bf16[32,1536]{1,0:T(8,128)(2,1)}, bf16[8,32,1536]{2,1,0:T(8,128)(2,1)}) custom-call(bf16[8,1536]{1,0:T(8,128)(2,1)} %act.1, bf16[1536,12288]{1,0:T(8,128)(2,1)} %weight.1, f32[1,12288]{1,0:T(1,128)} %bitcast.2, bf16[8,12288]{1,0:T(8,128)(2,1)} %cot.1), custom_call_target="tpu_custom_call" | custom-call | tf_op jit(solution)/shard_map/pallas_call | solution.py:287
  53.8 0.0 copy-start
  53.8 1.1 %copy-done = bf16[8,32,1536]{2,1,0:T(8,128)(2,1)S(1)} copy-done((bf16[8,32,1536]{2,1,0:T(8,128)(2,1)S(1)}, bf16[8,32,1536]{2,1,0:T(8,128)(2,1)}, u32[]{:S(2)}) %copy-start) | copy-done | bytes 786456
  54.9 0.0 copy-start.1
  54.9 0.9 %copy-done.1 = bf16[8,12288]{1,0:T(8,128)(2,1)S(1)} copy-done((bf16[8,12288]{1,0:T(8,128)(2,1)S(1)}, bf16[8,12288]{1,0:T(8,128)(2,1)}, u32[]{:S(2)}) %copy-start.1) | copy-done | bytes 196632
  55.8 0.0 copy-start.2
  55.8 0.9 %copy-done.2 = bf16[32,1536]{1,0:T(8,128)(2,1)S(1)} copy-done((bf16[32,1536]{1,0:T(8,128)(2,1)S(1)}, bf16[32,1536]{1,0:T(8,128)(2,1)}, u32[]{:S(2)}) %copy-start.2) | copy-done | bytes 98328
  56.7 0.0 copy-start.3
  56.7 0.7 copy-done.3
  57.5 25.1 %shard_map.76 = (bf16[1536,12288]{1,0:T(8,128)(2,1)}, f32[1,12288]{1,0:T(1,128)}, bf16[8,12288]{1,0:T(8,128)(2,1)}, bf16[8,1536]{1,0:T(8,128)(2,1)}) custom-call(bf16[32,1536]{1,0:T(8,128)(2,1)S(1)} %copy-done.2, bf16[8,32,1536]{2,1,0:T(8,128)(2,1)S(1)} %copy-done, bf16[8,12288]{1,0:T(8,128)(2,1)S(1)} %copy-done.1, bf16[8,1536]{1,0:T(8,128)(2,1)S(1)} %copy-done.3), custom_call_target="tpu_custom_call" | custom-call | tf_op jit(solution)/shard_map/pallas_call | solution.py:325
Async XLA Ops:
  53.8 1.1 %copy-start = (bf16[8,32,1536]{2,1,0:T(8,128)(2,1)S(1)}, bf16[8,32,1536]{2,1,0:T(8,128)(2,1)}, u32[]{:S(2)}) copy-start(bf16[8,32,1536]{2,1,0:T(8,128)(2,1)} %get-tuple-element.13.grad_ref) | copy-start | bytes 2359300
  54.9 0.9 %copy-start.1 = (bf16[8,12288]{1,0:T(8,128)(2,1)S(1)}, bf16[8,12288]{1,0:T(8,128)(2,1)}, u32[]{:S(2)}) copy-start(bf16[8,12288]{1,0:T(8,128)(2,1)} %get-tuple-element.14.hidden_in) | copy-start | bytes 589828
  55.8 0.9 %copy-start.2 = (bf16[32,1536]{1,0:T(8,128)(2,1)S(1)}, bf16[32,1536]{1,0:T(8,128)(2,1)}, u32[]{:S(2)}) copy-start(bf16[32,1536]{1,0:T(8,128)(2,1)} %get-tuple-element.12.x_ref) | copy-start | bytes 294916
  56.7 0.7 copy-start.3

commit v2 on v1

--- a/solution.py
+++ b/solution.py
@@ -145,31 +145,23 @@
     def g_out(k):
         return pltpu.make_async_copy(g32.at[k], grad_out.at[k], gout_sem.at[k])
 
-    tile = 512 if width % 512 == 0 else 256
-    ftile = 512 if feats % 512 == 0 else 256
-
     def dot_up(k):
         w_copy(k).wait()
 
-        def body(i, carry):
-            cols = pl.ds(pl.multiple_of(i * tile, tile), tile)
-            out = jnp.dot(x32[...], wbuf[k, :, cols], preferred_element_type=F32)
-            for j in range(4):
-                part[k, j % 2, j // 2, :, cols] = out[8 * j : 8 * j + 8]
-            return carry
-
-        lax.fori_loop(0, width // tile, body, 0)
+        out = jnp.dot(x32[...], wbuf[k], preferred_element_type=F32)
+        for j in range(4):
+            part[k, j % 2, j // 2] = out[8 * j : 8 * j + 8]
         s1_copy(k).start()
 
     def pair_sum(k):
         s1_copy(k).wait_recv()
-        s2[k] = part[k, core, 1 - x] + r1[k, 1 - x]
+        s2[k] = (part[k, core, 1 - x] + r1[k, 1 - x]).astype(BF16)
         s2_copy(k).start()
 
     def activate(k):
         s2_copy(k).wait_recv()
         cols = pl.ds(pl.multiple_of(k * width, 128), width)
-        pre = part[k, core, x] + r1[k, x] + r2[k] + bbuf[:, cols]
+        pre = part[k, core, x] + r1[k, x] + r2[k].astype(F32) + bbuf[:, cols]
         hbuf[:, cols] = gelu_tanh(pre).astype(BF16)
         gbuf[k, col] = (cbuf[:, cols].astype(F32) * gelu_slope(pre)).astype(BF16)
         gx_copy(k).start()
@@ -186,22 +178,17 @@
         g32[k] = grad
         g_out(k).start()
 
-        def body(i, carry):
-            feat = pl.ds(pl.multiple_of(i * ftile, ftile), ftile)
-            acc[:, feat] += lax.dot_general(
-                g32[k], wbuf[k, feat, :], (((1,), (1,)), ((), ())), preferred_element_type=F32
-            )
-            return carry
-
-        lax.fori_loop(0, feats // ftile, body, 0)
+        acc[...] += lax.dot_general(
+            grad, wbuf[k], (((1,), (1,)), ((), ())), preferred_element_type=F32
+        )
 
     def stages(t, carry):
-        for lag, stage in enumerate((dot_up, pair_sum, activate, forward, dot_down)):
+        for lag, stage in ((0, dot_up), (2, pair_sum), (4, activate), (6, forward), (8, dot_down)):
             k = t - lag
             pl.when(jnp.logical_and(k >= 0, k < chunks))(functools.partial(stage, k))
         return carry
 
-    lax.fori_loop(0, chunks + 4, stages, 0)
+    lax.fori_loop(0, chunks + 8, stages, 0)
 
     hidden_copy = pltpu.make_async_copy(hbuf, hidden_out, out_sem.at[1])
     hidden_copy.start()
@@ -261,17 +248,8 @@
         bias_ref[...] = jnp.sum(grad_ref[0].astype(F32), axis=0, keepdims=True)
 
     height = w_ref.shape[0]
-    step = 128
-
-    def body(n, carry):
-        at = pl.multiple_of(n * step, step)
-        lhs = xt[pl.ds(pl.multiple_of(i * height + at, step), step), :]
-        w_ref[pl.ds(at, step), :] = jnp.dot(
-            lhs, grad_ref[0], preferred_element_type=F32
-        ).astype(BF16)
-        return carry
-
-    lax.fori_loop(0, height // step, body, 0)
+    lhs = xt[pl.ds(pl.multiple_of(i * height, height), height), :]
+    w_ref[...] = jnp.dot(lhs, grad_ref[0], preferred_element_type=F32).astype(BF16)
 
     @pl.when(last)
     def _():
@@ -302,8 +280,8 @@
             pltpu.VMEM((1, hidden_units), F32),
             pltpu.VMEM((chunks, 2, 2, 8, width), F32),
             pltpu.VMEM((chunks, 2, 8, width), F32),
-            pltpu.VMEM((chunks, 8, width), F32),
-            pltpu.VMEM((chunks, 8, width), F32),
+            pltpu.VMEM((chunks, 8, width), BF16),
+            pltpu.VMEM((chunks, 8, width), BF16),
             pltpu.VMEM((chunks, 4, 8, width), BF16),
             pltpu.VMEM((chunks, 32, width), BF16),
             pltpu.VMEM((8, hidden_units), BF16),
@@ -321,7 +299,7 @@
         ),
     )(activations, up_weight, up_bias.reshape(1, hidden_units), cotangent)
 
-    split = 2
+    split = 1
     weight_grad, bias_grad, hidden, act_grad = pl.pallas_call(
         outer_kernel,
         grid=(chunks, split),
@@ -344,7 +322,7 @@
             any_spec,
         ),
         scratch_shapes=[pltpu.VMEM((feats, 32), BF16), dma((2,))],
-        compiler_params=pltpu.CompilerParams(vmem_limit_bytes=40 * 1024 * 1024),
+        compiler_params=pltpu.CompilerParams(vmem_limit_bytes=62 * 1024 * 1024),
     )(x_all, grad_all, hidden, act_grad)
     return hidden, act_grad, weight_grad, bias_grad.reshape(hidden_units)
 

time: 82.8 us -> 62.2 us (0.75)
  Pallas kernels: 78.2 us -> 61.5 us
  local copies, waits for them, and re-layouts: 3.68 us -> 0 us
    pallas_call x1, Pallas kernels: 53.1 us -> 44.5 us  [fast_per_device(): pl.pallas_call(functools.partial(exchange_kernel, chunks), out_shape=(jax...]
    pallas_call x1, Pallas kernels: 25.1 us -> 17 us  [fast_per_device(): pl.pallas_call(outer_kernel, grid=(chunks, split), out_shape=(jax.ShapeDt...]
    unnamed x8 -> x0, local copies, waits for them, and re-layouts: 3.68 us -> none
where the time goes in v2:
time: 62.2 us; the launch traced here: 62.1 us
  Pallas kernels  61.5 us (99%)
  between operations  0.64 us (1%)
    pallas_call x1, Pallas kernels, fast_per_device(): pl.pallas_call(functools.partial(exchange_kernel, chunks), out_shape=(jax...  44.5 us
    pallas_call x1, Pallas kernels, fast_per_device(): pl.pallas_call(outer_kernel, grid=(chunks, split), out_shape=(jax.ShapeDt...  17 us

profile of v2, /device:TPU:0, one launch (start us, length us, event | category | flops | bytes accessed | tf_op | source)
XLA Modules:
  0.0 62.1 jit_solution(9568211259338171453)
XLA Ops:
  0.6 44.5 %shard_map.75 = (bf16[8,12288]{1,0:T(8,128)(2,1)}, bf16[8,1536]{1,0:T(8,128)(2,1)}, bf16[32,1536]{1,0:T(8,128)(2,1)}, bf16[8,32,1536]{2,1,0:T(8,128)(2,1)}) custom-call(bf16[8,1536]{1,0:T(8,128)(2,1)} %act.1, bf16[1536,12288]{1,0:T(8,128)(2,1)} %weight.1, f32[1,12288]{1,0:T(1,128)} %bitcast.2, bf16[8,12288]{1,0:T(8,128)(2,1)} %cot.1), custom_call_target="tpu_custom_call" | custom-call | tf_op jit(solution)/shard_map/pallas_call | solution.py:265
  45.1 17.0 %shard_map.76 = (bf16[1536,12288]{1,0:T(8,128)(2,1)}, f32[1,12288]{1,0:T(1,128)}, bf16[8,12288]{1,0:T(8,128)(2,1)}, bf16[8,1536]{1,0:T(8,128)(2,1)}) custom-call(bf16[32,1536]{1,0:T(8,128)(2,1)} %get-tuple-element.12.x_ref, bf16[8,32,1536]{2,1,0:T(8,128)(2,1)} %get-tuple-element.13.grad_ref, bf16[8,12288]{1,0:T(8,128)(2,1)} %get-tuple-element.14.hidden_in, ...), custom_call_target="tpu_custom_call" | custom-call | tf_op jit(solution)/shard_map/pallas_call | solution.py:303
